TPU v7x, 32 devices: a whole 2x2x4 slice. The times are simulated.
32 devices in a mesh: sub: 4 (over z), row: 8 (over y, x, core).
Axes of the slice: x: 2, y: 2, z: 4, core: 2. Of those that a mesh axis runs over, the one named last changes fastest.
Arguments:
- spectra: bfloat16 [4, 65536, 256], P('sub', 'row')
- mass_blocks: bfloat16 [4, 512, 9, 128, 128], P('sub', 'row'), may hold values from -0.1875 to 0.1875
- offsets: int32 [4, 512, 9], P('sub', 'row'), may hold values from -16 to 16
- counts: int32 [4], P('sub'), may hold values from 1 to 65536, 183500 in all
Outputs:
- weighted_modes: bfloat16 [4, 65536, 192], P('sub', 'row')
Inputs may be any that keep to these rules, and one draw needn't show every extreme that they name: `counts`: rows at or past a subdomain's count hold no data; the largest count is exactly 65536.
All inputs are finite; a program needn't handle non-finite values. No bound on the sum of `counts` on one device may be relied on, other than what follows from the above.
Results may differ from a plain program's by a relative error of at most 0.001.
The roundings to bfloat16 on the way count: a program that leaves them out, or rounds other values in their place, can miss the bound.
Values may be sent and summed in bfloat16 or wider, within the bound.
A program may use at most 256 MiB of HBM per device.

v0:
```python
import functools

import jax
import jax.numpy as jnp
from jax import lax
from jax.experimental import pallas as pl
from jax.experimental.pallas import tpu as pltpu
from jax.sharding import PartitionSpec as P

RANK = 48
FREQ = 2
ITERS = 5
HB = 16
GROUP = 4
MESH = pl.DeviceIdType.MESH


def peer_copy(src, dst, send, recv, axis, index):
    return pltpu.make_async_remote_copy(
        src_ref=src, dst_ref=dst, send_sem=send, recv_sem=recv,
        device_id={axis: index}, device_id_type=MESH,
    )


def masked(value, rows, first, count):
    live = jnp.clip(count - first, 0, value.shape[0]).astype(jnp.float32)
    bound = jnp.full(value.shape, live, jnp.float32).astype(jnp.bfloat16)
    return jnp.where(rows < bound, value, jnp.zeros((), value.dtype))


def realify(part):
    width = part.shape[0]
    half = width // 2
    swapped = pltpu.roll(pltpu.roll(part, half, 0), half, 1)
    low_row = lax.broadcasted_iota(jnp.int32, part.shape, 0) < half
    low_col = lax.broadcasted_iota(jnp.int32, part.shape, 1) < half
    return swapped + jnp.where(low_row == low_col, part, -part)


def place(step, steps):
    edge, pair = HB // GROUP, HB // GROUP // 2
    inside = steps - 2 * edge
    late = step - inside
    turn = late // pair
    within = late % pair
    outer = jnp.where(
        turn == 0, steps - edge + within,
        jnp.where(turn == 1, pair + within, jnp.where(turn == 2, steps - pair + within, within)))
    return jnp.where(step < inside, step + edge, outer)


def weigh_kernel(
    n_row, n_sub, count_ref, offsets_ref, spectra_ref, mass_ref,
    weighted_ref, total_ref,
    own, low_near, low_far, high_near, high_far, rows_in, latest, gram, packed, landed, subs, gathered,
    load_sem, fill_sem, halo_send, halo_recv,
    first_send, first_recv, second_send, second_recv, third_send, third_recv,
):
    step = pl.program_id(0)
    steps = pl.num_programs(0)
    row = lax.axis_index("row")
    sub = lax.axis_index("sub")
    blocks, size, cols = own.shape
    reach = HB
    slots = mass_ref.shape[1]
    near = reach // 2
    pair = near // GROUP
    group = place(step, steps)
    count = count_ref[0]
    base = row * blocks
    after = lax.rem(row + 1, n_row)
    before = lax.rem(row + n_row - 1, n_row)

    def halo(src_at, dst, dst_at, sem, peer):
        return peer_copy(
            spectra_ref.at[pl.ds(src_at, near)], dst.at[pl.ds(dst_at, near)],
            halo_send.at[sem], halo_recv.at[sem], "row", peer)

    to_next = [halo(blocks - near, low_near, 0, 0, after),
               halo(blocks - reach, low_far, 0, 1, after)]
    to_prev = [halo(0, high_near, 2 * reach, 2, before),
               halo(near, high_far, 2 * reach, 3, before)]
    most = 2 * reach
    part = reach + near
    fills = [
        pltpu.make_async_copy(own.at[pl.ds(at, length)], buffer.at[pl.ds(to, length)],
                              fill_sem.at[sem])
        for sem, (at, length, buffer, to) in enumerate((
            (blocks - most, most, high_near, 0),
            (0, most, low_near, near),
            (blocks - part, part, high_far, 0),
            (0, part, low_far, reach),
        ))
    ]

    @pl.when(step == 0)
    def _():
        barrier = pltpu.get_barrier_semaphore()
        for j in range(1, n_row):
            pl.semaphore_signal(barrier, inc=1, device_id={"row": lax.rem(row + j, n_row)},
                                device_id_type=MESH)
        for j in range(1, n_sub):
            pl.semaphore_signal(barrier, inc=1, device_id={"sub": lax.rem(sub + j, n_sub)},
                                device_id_type=MESH)
        load = pltpu.make_async_copy(spectra_ref, own, load_sem)
        load.start()
        gram[...] = jnp.zeros_like(gram)
        latest[...] = jnp.zeros_like(latest)
        rows_in[...] = lax.broadcasted_iota(jnp.int32, (size, cols), 0).astype(
            jnp.float32).astype(jnp.bfloat16)

        @pl.when(row == 0)
        def _():
            low_near[pl.ds(0, near)] = jnp.zeros((near, size, cols), low_near.dtype)
            low_far[pl.ds(0, near)] = jnp.zeros((near, size, cols), low_far.dtype)

        @pl.when(row == n_row - 1)
        def _():
            high_near[pl.ds(most, near)] = jnp.zeros((near, size, cols), high_near.dtype)
            high_far[pl.ds(most, near)] = jnp.zeros((near, size, cols), high_far.dtype)

        pl.semaphore_wait(barrier, n_row + n_sub - 2)

        for at in range(2):
            @pl.when(row < n_row - 1)
            def _():
                to_next[at].start()

            @pl.when(row > 0)
            def _():
                to_prev[at].start()

        load.wait()

        def clear(b, carry):
            own[b] = masked(own[b], rows_in[...], (base + b) * size, count)
            return carry

        lax.fori_loop(0, blocks, clear, 0)
        for fill in fills:
            fill.start()

    def clear_halo(buffer, start, first_block, other=None, other_start=0):
        def body(b, carry):
            value = masked(buffer[start + b], rows_in[...], (first_block + b) * size, count)
            buffer[start + b] = value
            if other is not None:
                other[other_start + b] = value
            return carry
        lax.fori_loop(0, near, body, 0)

    inside = steps - 4 * pair

    @pl.when(step == inside)
    def _():
        @pl.when(row < n_row - 1)
        def _():
            to_prev[0].wait_recv()
        fills[0].wait()
        clear_halo(high_near, most, base + blocks, high_far, part)

    @pl.when(step == inside + pair)
    def _():
        @pl.when(row > 0)
        def _():
            to_next[0].wait_recv()
        fills[1].wait()
        clear_halo(low_near, 0, base - near, low_far, near)

    @pl.when(step == inside + 2 * pair)
    def _():
        @pl.when(row < n_row - 1)
        def _():
            to_prev[1].wait_recv()
        fills[2].wait()
        clear_halo(high_far, most, base + blocks + near)

    @pl.when(step == inside + 3 * pair)
    def _():
        @pl.when(row > 0)
        def _():
            to_next[1].wait_recv()
        fills[3].wait()
        clear_halo(low_far, 0, base - reach)

    def add_gram():
        z = latest[...]
        gram[...] += lax.dot_general(z, z, (((0,), (0,)), ((), ())),
                                     preferred_element_type=jnp.float32)

    def weigh(buffer, shift):
        fresh = []
        for r in range(GROUP):
            at = group * GROUP + r
            summed = None
            for k in range(0, slots, 2):
                ks = range(k, min(k + 2, slots))
                picks = [buffer[at + shift + offsets_ref[k, 0, at]] for k in ks]
                product = jnp.dot(
                    jnp.concatenate([mass_ref[r, k] for k in ks], axis=1),
                    jnp.concatenate(picks, axis=0), preferred_element_type=jnp.float32)
                summed = product if summed is None else summed + product
            value = masked(summed.astype(weighted_ref.dtype), rows_in[...],
                           (base + at) * size, count)
            weighted_ref[r] = value
            fresh.append(value)
        add_gram()
        latest[...] = jnp.concatenate(fresh, axis=0)

    for least, buffer, shift in (
        (0, own, 0),
        (1, high_near, most - blocks),
        (2, low_near, near),
        (3, high_far, part - blocks),
        (4, low_far, reach),
    ):
        first = 0 if least == 0 else inside + (least - 1) * pair
        last = inside + least * pair

        @pl.when(jnp.logical_and(step >= first, step < last))
        def _():
            weigh(buffer, shift)

    @pl.when(step == steps - 1)
    def _():
        add_gram()
        width = cols // FREQ
        depth = packed.shape[1]
        for f in range(FREQ):
            cut = slice(f * width, (f + 1) * width)
            top = realify(gram[cut, cut])[: width // 2]
            pieces = (width // 2) // depth
            packed[f * pieces : (f + 1) * pieces] = top.reshape(pieces, depth, width)

        def spread(n, axis, me, src, slot_of, send, recv):
            copies = []
            for j in range(1, n):
                peer = lax.rem(me + j, n)
                copy = peer_copy(src(peer), slot_of(me), send.at[j], recv.at[j], axis, peer)
                copy.start()
                copies.append(copy)
            for j in range(1, n):
                peer = lax.rem(me + n - j, n)
                peer_copy(src(peer), slot_of(peer), send.at[j], recv.at[j], axis, peer).wait_recv()
            return copies

        first = spread(n_row, "row", row, lambda p: packed.at[p], lambda s: landed.at[s],
                       first_send, first_recv)
        landed[row] = packed[row]
        partial = landed[0]
        for j in range(1, n_row):
            partial = partial + landed[j]
        subs[sub] = partial
        second = spread(n_sub, "sub", sub, lambda p: subs.at[sub], lambda s: subs.at[s],
                        second_send, second_recv)
        whole = subs[0]
        for j in range(1, n_sub):
            whole = whole + subs[j]
        gathered[row] = whole
        third = spread(n_row, "row", row, lambda p: gathered.at[row], lambda s: gathered.at[s],
                       third_send, third_recv)
        total_ref[...] = gathered[...]

        for at in range(2):
            @pl.when(row < n_row - 1)
            def _():
                to_next[at].wait_send()

            @pl.when(row > 0)
            def _():
                to_prev[at].wait_send()

        for copy in first + second + third:
            copy.wait_send()


def weigh_call(n_row, n_sub, counts, offsets, spectra, mass_blocks):
    blocks, size, cols = spectra.shape
    slots = mass_blocks.shape[1]
    steps = blocks // GROUP
    window = 2 * HB + HB // 2
    width = cols // FREQ
    depth = FREQ * (width // 2) // n_row
    dma = pltpu.SemaphoreType.DMA

    return pl.pallas_call(
        functools.partial(weigh_kernel, n_row, n_sub),
        grid=(steps,),
        out_shape=(
            jax.ShapeDtypeStruct((blocks, size, cols), jnp.bfloat16),
            jax.ShapeDtypeStruct((n_row, depth, width), jnp.float32),
        ),
        in_specs=[
            pl.BlockSpec(memory_space=pltpu.SMEM),
            pl.BlockSpec(memory_space=pltpu.SMEM),
            pl.BlockSpec(memory_space=pltpu.HBM),
            pl.BlockSpec((GROUP, slots, size, size), lambda i: (place(i, steps), 0, 0, 0)),
        ],
        out_specs=(
            pl.BlockSpec((GROUP, size, cols), lambda i: (place(i, steps), 0, 0)),
            pl.BlockSpec(memory_space=pltpu.VMEM),
        ),
        scratch_shapes=[
            pltpu.VMEM((blocks, size, cols), jnp.bfloat16),
            pltpu.VMEM((window, size, cols), jnp.bfloat16),
            pltpu.VMEM((window, size, cols), jnp.bfloat16),
            pltpu.VMEM((window, size, cols), jnp.bfloat16),
            pltpu.VMEM((window, size, cols), jnp.bfloat16),
            pltpu.VMEM((size, cols), jnp.bfloat16),
            pltpu.VMEM((GROUP * size, cols), jnp.bfloat16),
            pltpu.VMEM((cols, cols), jnp.float32),
            pltpu.VMEM((n_row, depth, width), jnp.float32),
            pltpu.VMEM((n_row, depth, width), jnp.float32),
            pltpu.VMEM((n_sub, depth, width), jnp.float32),
            pltpu.VMEM((n_row, depth, width), jnp.float32),
            dma, dma((4,)), dma((4,)), dma((4,)),
            dma((n_row,)), dma((n_row,)),
            dma((n_sub,)), dma((n_sub,)),
            dma((n_row,)), dma((n_row,)),
        ],
        compiler_params=pltpu.CompilerParams(
            collective_id=0, has_side_effects=True, vmem_limit_bytes=60 << 20,
            dimension_semantics=("arbitrary",),
        ),
        name="weigh",
    )(counts, offsets, spectra, mass_blocks)


def spot(shape, shift, least, most):
    source = lax.broadcasted_iota(jnp.int32, shape, 0)
    target = lax.broadcasted_iota(jnp.int32, shape, 1)
    hit = (target == source + shift) & (source >= least) & (source < most)
    return jnp.where(hit, 1.0, 0.0).astype(jnp.bfloat16)


def halves(value):
    head = value.astype(jnp.bfloat16)
    return head, (value - head.astype(jnp.float32)).astype(jnp.bfloat16)


def exact(first, second):
    a, a_rest = halves(first)
    b, b_rest = halves(second)
    return jnp.dot(
        jnp.concatenate([a, a, a_rest], axis=1), jnp.concatenate([b, b_rest, b], axis=0),
        preferred_element_type=jnp.float32)


def project_kernel(top_ref, z_ref, modes_ref, projector):
    @pl.when(pl.program_id(0) == 0)
    def _():
        width = top_ref.shape[1]
        half = width // 2
        out_cols = projector.shape[0]
        rows = lax.broadcasted_iota(jnp.int32, (width, width), 0)
        columns = lax.broadcasted_iota(jnp.int32, (width, width), 1)
        lift = jnp.where(rows == columns, 1.5, 0.0)
        iterates = []
        for f in range(FREQ):
            top = top_ref[f * half : (f + 1) * half]
            bottom = pltpu.roll(top, half, 1)
            bottom = jnp.where(columns[:half] < half, -bottom, bottom)
            full = jnp.concatenate([top, bottom], axis=0)
            norm = jnp.sqrt(jnp.sum(full * full, axis=(0, 1), keepdims=True) + 1e-06)
            iterates.append(full / norm)
        whiteners = [None] * FREQ
        for at in range(ITERS):
            for f in range(FREQ):
                both = iterates[f] if at == 0 else exact(whiteners[f], iterates[f])
                fix = lift - 0.5 * both
                if at < ITERS - 1:
                    iterates[f] = exact(iterates[f], fix)
                whiteners[f] = fix if at == 0 else exact(fix, whiteners[f])
        for f in range(FREQ):
            straight = jnp.where(rows < half, whiteners[f], -whiteners[f])
            crossed = pltpu.roll(whiteners[f], half, 0)
            shape = (width, out_cols)
            value = jnp.dot(
                straight.astype(jnp.bfloat16), spot(shape, 2 * f * RANK, 0, RANK),
                preferred_element_type=jnp.float32)
            value += jnp.dot(
                crossed.astype(jnp.bfloat16), spot(shape, (2 * f + 1) * RANK, 0, RANK),
                preferred_element_type=jnp.float32)
            projector[:, f * width : (f + 1) * width] = value.T.astype(jnp.bfloat16)

    modes_ref[...] = lax.dot_general(
        projector[...], z_ref[...], (((1,), (1,)), ((), ())),
        preferred_element_type=jnp.float32).astype(modes_ref.dtype)


def project_call(top, weighted):
    rows, cols = weighted.shape
    out_cols = FREQ * 2 * RANK
    tile = 1024
    return pl.pallas_call(
        project_kernel,
        grid=(rows // tile,),
        out_shape=jax.ShapeDtypeStruct((out_cols, rows), jnp.bfloat16),
        in_specs=[
            pl.BlockSpec(top.shape, lambda i: (0, 0)),
            pl.BlockSpec((tile, cols), lambda i: (i, 0)),
        ],
        out_specs=pl.BlockSpec((out_cols, tile), lambda i: (0, i)),
        scratch_shapes=[pltpu.VMEM((out_cols, cols), jnp.bfloat16)],
        compiler_params=pltpu.CompilerParams(
            vmem_limit_bytes=60 << 20, dimension_semantics=("arbitrary",)),
        name="project",
    )(top, weighted)


def local(n_row, n_sub, spectra, mass_blocks, offsets, counts):
    rows, cols = spectra.shape[1:]
    size = mass_blocks.shape[3]
    weighted, total = weigh_call(
        n_row, n_sub, counts, offsets.transpose(2, 0, 1),
        spectra[0].reshape(rows // size, size, cols), mass_blocks[0])
    width = cols // FREQ
    modes = project_call(
        total.reshape(FREQ * width // 2, width), weighted.reshape(rows, cols))
    return modes.T[None]


def solution(mesh):
    return jax.shard_map(
        functools.partial(local, mesh.shape["row"], mesh.shape["sub"]),
        mesh=mesh,
        in_specs=(
            P("sub", "row", None),
            P("sub", "row", None, None, None),
            P("sub", "row", None),
            P("sub"),
        ),
        out_specs=P("sub", "row", None),
        check_vma=False,
    )
```

profile of v0, /device:TPU:0, one launch (start us, length us, event | category | flops | bytes accessed | tf_op | source)
XLA Modules:
  0.0 56.3 jit_solution(7934510083973342106)
XLA Ops:
  0.7 45.8 %weigh.1 = (bf16[64,128,256]{2,1,0:T(8,128)(2,1)}, f32[8,16,128]{2,1,0:T(8,128)}) custom-call(s32[1]{0:T(128)S(6)} %copy.5.count_ref, s32[9,1,64]{2,1,0:T(1,128)} %bitcast.12, bf16[64,128,256]{2,1,0:T(8,128)(2,1)} %bitcast.9, bf16[64,9,128,128]{3,2,1,0:T(8,128)(2,1)} %bitcast.8), custom_call_target="tpu_custom_call" | custom-call | tf_op jit(solution)/shard_map/weigh/pallas_call | solution.py:286
  46.4 9.9 %project.1 = bf16[192,8192]{1,0:T(8,128)(2,1)} custom-call(f32[128,128]{1,0:T(8,128)} %bitcast.11, bf16[8192,256]{1,0:T(8,128)(2,1)} %bitcast.10), custom_call_target="tpu_custom_call" | custom-call | tf_op jit(solution)/shard_map/project/pallas_call | solution.py:395
where the time goes:
time: 57 us; the launch traced here: 56.3 us
  Pallas kernels  55.7 us (98%)
  between operations  0.66 us (1%)
    pallas_call x1, Pallas kernels, weigh_call(): pl.pallas_call(functools.partial(weigh_kernel, n_row, n_sub), grid=(steps...  45.8 us
    pallas_call x1, Pallas kernels, project_call(): pl.pallas_call(project_kernel, grid=(rows // tile,), out_shape=jax.ShapeD...  9.88 us

commit v1 on v0

--- a/solution.py
+++ b/solution.py
@@ -52,8 +52,8 @@
 def weigh_kernel(
     n_row, n_sub, count_ref, offsets_ref, spectra_ref, mass_ref,
     weighted_ref, total_ref,
-    own, low_near, low_far, high_near, high_far, rows_in, latest, gram, packed, landed, subs, gathered,
-    load_sem, fill_sem, halo_send, halo_recv,
+    own, low_near, low_far, high_near, high_far, rows_in, relay, latest, gram, packed, landed, subs, gathered,
+    load_sem, relay_send, relay_recv, fill_sem, halo_send, halo_recv,
     first_send, first_recv, second_send, second_recv, third_send, third_recv,
 ):
     step = pl.program_id(0)
@@ -82,6 +82,21 @@
                halo(near, high_far, 2 * reach, 3, before)]
     most = 2 * reach
     part = reach + near
+    relays = [(3, 7, 4), (4, 0, 3)] if n_row == 8 else []
+    direct = [row < n_row - 1, row > 0]
+    for source, via, goal in relays:
+        side = 0 if goal > source else 1
+        direct[side] = jnp.logical_and(direct[side], row != source)
+    sends = [(to_next[0], row < n_row - 1), (to_prev[0], row > 0)]
+    onward = []
+    for source, via, goal in relays:
+        at = blocks - reach if goal > source else near
+        into = peer_copy(spectra_ref.at[pl.ds(at, near)], relay, relay_send, relay_recv, "row", via)
+        sends.append((into, row == source))
+        far, to, sem = (low_far, 0, 1) if goal > source else (high_far, most, 3)
+        onward.append((via, into, peer_copy(
+            relay, far.at[pl.ds(to, near)], halo_send.at[sem], halo_recv.at[sem], "row", goal)))
+    sends += [(to_next[1], direct[0]), (to_prev[1], direct[1])]
     fills = [
         pltpu.make_async_copy(own.at[pl.ds(at, length)], buffer.at[pl.ds(to, length)],
                               fill_sem.at[sem])
@@ -121,14 +136,10 @@
 
         pl.semaphore_wait(barrier, n_row + n_sub - 2)
 
-        for at in range(2):
-            @pl.when(row < n_row - 1)
+        for copy, mine in sends:
+            @pl.when(mine)
             def _():
-                to_next[at].start()
-
-            @pl.when(row > 0)
-            def _():
-                to_prev[at].start()
+                copy.start()
 
         load.wait()
 
@@ -150,6 +161,14 @@
         lax.fori_loop(0, near, body, 0)
 
     inside = steps - 4 * pair
+
+    @pl.when(step == inside - 3)
+    def _():
+        for via, into, forward in onward:
+            @pl.when(row == via)
+            def _():
+                into.wait_recv()
+                forward.start()
 
     @pl.when(step == inside)
     def _():
@@ -261,14 +280,10 @@
                        third_send, third_recv)
         total_ref[...] = gathered[...]
 
-        for at in range(2):
-            @pl.when(row < n_row - 1)
+        for copy, mine in sends + [(forward, row == via) for via, into, forward in onward]:
+            @pl.when(mine)
             def _():
-                to_next[at].wait_send()
-
-            @pl.when(row > 0)
-            def _():
-                to_prev[at].wait_send()
+                copy.wait_send()
 
         for copy in first + second + third:
             copy.wait_send()
@@ -307,13 +322,14 @@
             pltpu.VMEM((window, size, cols), jnp.bfloat16),
             pltpu.VMEM((window, size, cols), jnp.bfloat16),
             pltpu.VMEM((size, cols), jnp.bfloat16),
+            pltpu.VMEM((HB // 2, size, cols), jnp.bfloat16),
             pltpu.VMEM((GROUP * size, cols), jnp.bfloat16),
             pltpu.VMEM((cols, cols), jnp.float32),
             pltpu.VMEM((n_row, depth, width), jnp.float32),
             pltpu.VMEM((n_row, depth, width), jnp.float32),
             pltpu.VMEM((n_sub, depth, width), jnp.float32),
             pltpu.VMEM((n_row, depth, width), jnp.float32),
-            dma, dma((4,)), dma((4,)), dma((4,)),
+            dma, dma, dma, dma((4,)), dma((4,)), dma((4,)),
             dma((n_row,)), dma((n_row,)),
             dma((n_sub,)), dma((n_sub,)),
             dma((n_row,)), dma((n_row,)),
@@ -346,9 +362,11 @@
         preferred_element_type=jnp.float32)
 
 
-def project_kernel(top_ref, z_ref, modes_ref, projector):
+def project_kernel(top_ref, weighted_ref, modes_ref, projector, z_ref, load_sem):
     @pl.when(pl.program_id(0) == 0)
     def _():
+        load = pltpu.make_async_copy(weighted_ref, z_ref, load_sem)
+        load.start()
         width = top_ref.shape[1]
         half = width // 2
         out_cols = projector.shape[0]
@@ -382,9 +400,13 @@
                 crossed.astype(jnp.bfloat16), spot(shape, (2 * f + 1) * RANK, 0, RANK),
                 preferred_element_type=jnp.float32)
             projector[:, f * width : (f + 1) * width] = value.T.astype(jnp.bfloat16)
+        load.wait()
+
+    tile = modes_ref.shape[1]
+    at = pl.multiple_of(pl.program_id(0) * tile, tile)
 
     modes_ref[...] = lax.dot_general(
-        projector[...], z_ref[...], (((1,), (1,)), ((), ())),
+        projector[...], z_ref[pl.ds(at, tile)], (((1,), (1,)), ((), ())),
         preferred_element_type=jnp.float32).astype(modes_ref.dtype)
 
 
@@ -398,10 +420,14 @@
         out_shape=jax.ShapeDtypeStruct((out_cols, rows), jnp.bfloat16),
         in_specs=[
             pl.BlockSpec(top.shape, lambda i: (0, 0)),
-            pl.BlockSpec((tile, cols), lambda i: (i, 0)),
+            pl.BlockSpec(memory_space=pl.ANY),
         ],
         out_specs=pl.BlockSpec((out_cols, tile), lambda i: (0, i)),
-        scratch_shapes=[pltpu.VMEM((out_cols, cols), jnp.bfloat16)],
+        scratch_shapes=[
+            pltpu.VMEM((out_cols, cols), jnp.bfloat16),
+            pltpu.VMEM((rows, cols), jnp.bfloat16),
+            pltpu.SemaphoreType.DMA,
+        ],
         compiler_params=pltpu.CompilerParams(
             vmem_limit_bytes=60 << 20, dimension_semantics=("arbitrary",)),
         name="project",

time: 57 us -> 49.2 us (0.86)
  Pallas kernels: 55.7 us -> 47.9 us
    pallas_call x1, Pallas kernels: 45.8 us -> 39.9 us  [weigh_call(): pl.pallas_call(functools.partial(weigh_kernel, n_row, n_sub), grid=(steps...]
    pallas_call x1, Pallas kernels: 9.88 us -> 7.99 us  [project_call(): pl.pallas_call(project_kernel, grid=(rows // tile,), out_shape=jax.ShapeD...]
where the time goes in v1:
time: 49.2 us; the launch traced here: 48.6 us
  Pallas kernels  47.9 us (97%)
  between operations  0.66 us (1%)
    pallas_call x1, Pallas kernels, weigh_call(): pl.pallas_call(functools.partial(weigh_kernel, n_row, n_sub), grid=(steps...  39.9 us
    pallas_call x1, Pallas kernels, project_call(): pl.pallas_call(project_kernel, grid=(rows // tile,), out_shape=jax.ShapeD...  7.99 us

profile of v1, /device:TPU:0, one launch (start us, length us, event | category | flops | bytes accessed | tf_op | source)
XLA Modules:
  0.0 48.6 jit_solution(14647157005650159925)
XLA Ops:
  0.7 39.9 %weigh.1 = (bf16[64,128,256]{2,1,0:T(8,128)(2,1)}, f32[8,16,128]{2,1,0:T(8,128)}) custom-call(s32[1]{0:T(128)S(6)} %copy.5.count_ref, s32[9,1,64]{2,1,0:T(1,128)} %bitcast.12, bf16[64,128,256]{2,1,0:T(8,128)(2,1)} %bitcast.9, bf16[64,9,128,128]{3,2,1,0:T(8,128)(2,1)} %bitcast.8), custom_call_target="tpu_custom_call" | custom-call | tf_op jit(solution)/shard_map/weigh/pallas_call | solution.py:301
  40.6 8.0 %project.1 = bf16[192,8192]{1,0:T(8,128)(2,1)} custom-call(f32[128,128]{1,0:T(8,128)} %bitcast.11, bf16[8192,256]{1,0:T(8,128)(2,1)} %bitcast.10), custom_call_target="tpu_custom_call" | custom-call | tf_op jit(solution)/shard_map/project/pallas_call | solution.py:417
